TPU v7x, 32 devices: a whole 2x2x4 slice. The times are simulated.
32 devices in a mesh: rows: 16 (over z, y, x), rep: 2 (over core).
Axes of the slice: x: 2, y: 2, z: 4, core: 2. Of those that a mesh axis runs over, the one named last changes fastest.
Arguments:
- entity_table: bfloat16 [98304, 256], P('rows'), may hold values from -3 to 3
- relation_ops: bfloat16 [8, 256, 256], replicated, may hold values from -0.375 to 0.375
- need_rows: int32 [16, 2, 16, 8], P('rows', 'rep'), may hold values from 0 to 6143
- send_offsets: int32 [16, 2, 17], P('rows', 'rep'), may hold values from 0 to 128, as said below
- source_ids: int32 [16, 2, 2, 1024], P('rows', 'rep'), may hold values from 0 to 127, as said below
- target_ids: int32 [16, 2, 2, 1024], P('rows', 'rep'), may hold values from 0 to 127, as said below
- negative_ids: int32 [16, 2, 2, 1024], P('rows', 'rep'), may hold values from 0 to 127, as said below
- relation_ids: int32 [16, 2, 2], P('rows', 'rep'), may hold values from 0 to 7
Outputs:
- entity_grad: bfloat16 [98304, 256], P(('rows', 'rep'))
- relation_grad: float32 [8, 256, 256], replicated
Inputs may be any that keep to these rules, and one draw needn't show every extreme that they name: `send_offsets`: along the last dimension the offsets start at 0 and rise by 2 to 8 from owner to owner; there is one owner, the same for every device, from which every device requests exactly 8 rows (rise of 8), and there is one device that requests 8 rows from every owner. `source_ids`: each id is below the device's last entry of send_offsets; on every device some id is 0 and some id is that last entry minus 1. `target_ids`: each id is below the device's last entry of send_offsets; on every device some id is 0 and some id is that last entry minus 1. `negative_ids`: each id is below the device's last entry of send_offsets; on every device some id is 0 and some id is that last entry minus 1. `need_rows`: entries past an owner's count of requested rows are not referenced.
All inputs are finite; a program needn't handle non-finite values.
Results may differ from a plain program's by a relative error of at most 0.0065.
Values may be sent and summed in bfloat16 or wider, within the bound.
A program may use at most 64 MiB of HBM per device.

v0:
```python
import jax
import jax.numpy as jnp
from jax import lax
from jax.sharding import PartitionSpec as P


def locate(edge_ids, offsets, capacity):
    upper_bound = offsets[1:]
    lower_bound = offsets[:-1]
    owner_index = jnp.sum((edge_ids[..., None] >= upper_bound).astype(jnp.int32), axis=-1)
    start_slot = jnp.max(jnp.where(edge_ids[..., None] >= lower_bound, lower_bound, 0), axis=-1)
    return owner_index * capacity + edge_ids - start_slot


def block_terms(source, target, negative, operator, weight_neg):
    query = jnp.dot(source, operator, preferred_element_type=jnp.float32).astype(jnp.bfloat16)
    positive = jnp.einsum("bd,bd->b", query, target, preferred_element_type=jnp.float32)
    scores = jnp.einsum("bd,nd->bn", query, negative, preferred_element_type=jnp.float32)
    slope = -jax.nn.sigmoid(-positive)
    neg_weight = (jax.nn.sigmoid(scores) * weight_neg).astype(jnp.bfloat16)
    query_grad = slope[:, None] * target.astype(jnp.float32) + jnp.dot(
        neg_weight, negative, preferred_element_type=jnp.float32
    )
    query_grad = query_grad.astype(jnp.bfloat16)
    target_grad = slope[:, None] * query.astype(jnp.float32)
    negative_grad = jnp.einsum("bn,bd->nd", neg_weight, query, preferred_element_type=jnp.float32)
    source_grad = jnp.einsum("bd,ed->be", query_grad, operator, preferred_element_type=jnp.float32)
    operator_grad = jnp.einsum("be,bd->ed", source, query_grad, preferred_element_type=jnp.float32)
    return (source_grad, target_grad, negative_grad, operator_grad)


def shards(
    entity_table,
    relation_ops,
    need_rows,
    send_offsets,
    source_ids,
    target_ids,
    negative_ids,
    relation_ids,
):
    requests = need_rows[0, 0]
    owner_count, capacity = requests.shape
    row_width = entity_table.shape[1]
    received = lax.all_to_all(requests, "rows", split_axis=0, concat_axis=0, tiled=True)
    serve_picked = jnp.take(entity_table, received, axis=0)
    returned = lax.all_to_all(serve_picked, "rows", split_axis=0, concat_axis=0, tiled=True)
    fetched = returned
    slot_count = owner_count * capacity
    slots = fetched.reshape(slot_count, row_width)
    offsets = send_offsets[0, 0]
    source_slot = locate(source_ids[0, 0], offsets, capacity)
    target_slot = locate(target_ids[0, 0], offsets, capacity)
    negative_slot = locate(negative_ids[0, 0], offsets, capacity)
    relations = relation_ids[0, 0]
    edge_count = source_ids.shape[-1]
    weight_neg = negative_ids.shape[-1] ** (-0.5)
    slot_lane = jnp.arange(slot_count, dtype=jnp.int32)
    relation_lane = jnp.arange(relation_ops.shape[0], dtype=jnp.int32)
    slot_grad = jnp.zeros((slot_count, row_width), jnp.float32)
    operator_acc = jnp.zeros(relation_ops.shape, jnp.float32)
    for block_index in range(relations.shape[0]):
        joined_slot = jnp.concatenate(
            [source_slot[block_index], target_slot[block_index], negative_slot[block_index]], axis=0
        )
        picker = (joined_slot[:, None] == slot_lane[None, :]).astype(jnp.bfloat16)
        picked = jnp.dot(picker, slots, preferred_element_type=jnp.float32).astype(jnp.bfloat16)
        source = picked[:edge_count]
        target = picked[edge_count : 2 * edge_count]
        negative = picked[2 * edge_count :]
        operator = lax.dynamic_index_in_dim(relation_ops, relations[block_index], 0, keepdims=False)
        source_grad, target_grad, negative_grad, operator_grad = block_terms(
            source, target, negative, operator, weight_neg
        )
        joined_grad = jnp.concatenate([source_grad, target_grad, negative_grad], axis=0)
        upper_part = joined_grad.astype(jnp.bfloat16)
        lower_part = (joined_grad - upper_part.astype(jnp.float32)).astype(jnp.bfloat16)
        slot_grad = slot_grad + jnp.einsum(
            "rs,rd->sd", picker, upper_part, preferred_element_type=jnp.float32
        )
        slot_grad = slot_grad + jnp.einsum(
            "rs,rd->sd", picker, lower_part, preferred_element_type=jnp.float32
        )
        chosen = (relation_lane == relations[block_index]).astype(jnp.float32)
        operator_acc = operator_acc + chosen[:, None, None] * operator_grad[None, :, :]
    operator_total = lax.psum(operator_acc, ("rows", "rep"))
    devices = lax.axis_size("rows") * lax.axis_size("rep")
    relation_grad = (
        operator_total
        * (relation_ops.shape[0] / (edge_count * relations.shape[0] * devices)) ** 0.5
    )
    returned = lax.all_to_all(
        slot_grad.reshape(owner_count, capacity, row_width),
        "rows",
        split_axis=0,
        concat_axis=0,
        tiled=True,
    )
    flat_index = received.reshape(-1)
    flat_grad = returned.reshape(-1, row_width)
    owner_slab = (
        jnp.zeros((entity_table.shape[0], row_width), jnp.float32).at[flat_index].add(flat_grad)
    )
    entity_grad = lax.psum_scatter(owner_slab, "rep", scatter_dimension=0, tiled=True)
    return (entity_grad.astype(jnp.bfloat16), relation_grad)


def solution(mesh):
    return jax.shard_map(
        shards,
        mesh=mesh,
        in_specs=(
            P("rows", None),
            P(),
            P("rows", "rep", None, None),
            P("rows", "rep", None),
            P("rows", "rep", None, None),
            P("rows", "rep", None, None),
            P("rows", "rep", None, None),
            P("rows", "rep", None),
        ),
        out_specs=(P(("rows", "rep"), None), P()),
        check_vma=False,
    )
```

profile of v0, /device:TPU:1, one launch (start us, length us, event | category | flops | bytes accessed | tf_op | source)
XLA Modules:
  0.0 205.4 jit_solution(2638052348424822502)
XLA Ops:
  8.0 0.0 copy-start
  8.0 1.5 copy.21
  9.5 7.4 %all-to-all-start = ((s32[16,1,8]{2,1,0:T(1,128)}), s32[16,1,8]{2,1,0:T(1,128)S(1)}, u32[]{:S(2)}, u32[]{:S(2)}) async-start(s32[16,1,8]{2,1,0:T(1,128)} %copy.21), calls=%async_computation | async-start | bytes 16384 | tf_op jit(solution)/shard_map/all_to_all | solution.py:45
  16.9 0.8 slice_bitcast_fusion
  17.7 1.0 convert_reduce_fusion
  18.8 0.7 add_subtract_fusion
  19.5 0.7 add_subtract_fusion.2
  20.3 1.4 fusion.69
  21.7 1.3 all-to-all-done
  23.0 0.1 copy.22
  23.1 0.1 copy.23
  23.2 0.1 copy.25
  23.2 0.1 reshape.115
  23.3 0.0 copy-done
  23.3 0.8 gather_fusion
  24.2 0.7 bitcast_select_fusion
  24.9 5.0 %all-to-all-start.1 = ((bf16[16,8,256]{2,1,0:T(8,128)(2,1)}), bf16[16,8,256]{2,1,0:T(8,128)(2,1)S(1)}, u32[]{:S(2)}, u32[]{:S(2)}) async-start(bf16[16,8,256]{2,1,0:T(8,128)(2,1)} %bitcast_select_fusion), calls=%async_computation.1 | async-start | bytes 131072 | tf_op jit(solution)/shard_map/all_to_all | solution.py:47
  29.9 0.0 all-reduce.2.cloned.1.call-start
  30.0 1.3 compare_convert_fusion
  35.4 1.1 all-to-all-done.1
  36.4 1.6 convolution_convert_fusion.1
  38.1 1.3 fusion.26
  39.4 0.0 copy-start.3
  39.4 1.3 multiply_convert_fusion.1
  40.7 0.0 copy-done.3
  40.7 0.0 copy-start.4
  40.7 1.3 convert_multiply_fusion.2
  42.0 0.7 fusion.12
  42.8 0.0 copy-done.4
  42.8 0.3 fusion.41
  43.1 2.2 %fusion.48 = f32[1024,256]{1,0:T(8,128)} fusion(bf16[1024,256]{1,0:T(8,128)(2,1)S(1)} %fusion.12, bf16[8,256,256]{2,1,0:T(8,128)(2,1)} %param.9, s32[]{:T(128)S(6)} %select_n.54), kind=kOutput, calls=%fused_computation.60 | convolution fusion | flops 134217728 | bytes 1703940 | tf_op jit(solution)/shard_map/bd,ed->be/dot_general | solution.py:27
  45.3 1.8 convolution_convert_fusion
  47.2 1.3 fusion.27
  48.5 1.3 multiply_convert_fusion
  49.8 0.2 convert_multiply_fusion
  50.0 0.7 fusion.13
  50.7 0.7 fusion.71
  51.5 0.3 fusion.36
  51.8 1.2 fusion.45
  53.1 1.1 fusion.4
  54.1 1.1 fusion.5
  55.2 1.7 multiply_add_fusion
  56.9 0.0 all-reduce.2.cloned.1.call-update
  57.0 0.0 copy-start.1
  57.0 0.0 copy-start.2
  57.0 2.6 %fusion.70 = f32[1024,256]{1,0:T(8,128)S(1)} fusion(bf16[1024,1024]{1,0:T(8,128)(2,1)} %copy-done.4, bf16[1024,256]{1,0:T(8,128)(2,1)} %copy-done.3), kind=kOutput, calls=%fused_computation.105 | convolution fusion | flops 536870912 | bytes 3670016 | tf_op jit(solution)/shard_map/bn,bd->nd/dot_general | solution.py:26
  59.5 0.0 copy-done.1
  59.5 0.0 copy-done.2
  59.6 1.1 fusion.6
  60.6 1.7 fusion.23
  62.4 5.3 %all-to-all-start.2 = ((f32[16,8,256]{2,1,0:T(8,128)}), f32[16,8,256]{2,1,0:T(8,128)S(1)}, u32[]{:S(2)}, u32[]{:S(2)}) async-start(f32[16,8,256]{2,1,0:T(8,128)} %fusion.23), calls=%async_computation.2 | async-start | bytes 262144 | tf_op jit(solution)/shard_map/all_to_all | solution.py:92
  67.7 0.0 reduce-scatter.2.cloned.1.call-start
  67.7 0.5 broadcast.84
  68.2 0.7 reduce.7
  68.9 0.1 reshape.109
  69.0 6.0 %all-to-all-done.2 = f32[16,8,256]{2,1,0:T(8,128)S(1)} async-done(((f32[16,8,256]{2,1,0:T(8,128)}), f32[16,8,256]{2,1,0:T(8,128)S(1)}, u32[]{:S(2)}, u32[]{:S(2)}) %all-to-all-start.2) | async-done | bytes 131104 | tf_op jit(solution)/shard_map/all_to_all | solution.py:92
  75.0 4.3 %scatter_custom_fusion = f32[6144,256]{1,0:T(8,128)} fusion(s32[128]{0:T(128)S(1)} %fusion.57, f32[]{:T(128)} %constant.10.clone.1, f32[16,8,256]{2,1,0:T(8,128)S(1)} %all-to-all-done.2), kind=kCustom, calls=%fused_computation.10 | custom fusion | flops 32768 | bytes 6422532 | tf_op jit(solution)/shard_map/scatter-add | solution.py:102
  79.3 0.0 reduce-scatter.2.cloned.1.call-update
  79.3 112.3 %all-reduce.2.cloned.1.call-done = f32[8,256,256]{2,1,0:T(8,128)} async-done(((f32[8,256,256]{2,1,0:T(8,128)}), f32[8,256,256]{2,1,0:T(8,128)}) %all-reduce.2.cloned.1.call-update) | async-done | bytes 2097168 | tf_op jit(solution)/shard_map/psum | solution.py:86
  191.7 3.1 %broadcast_multiply_fusion = f32[8,256,256]{2,1,0:T(8,128)} fusion(f32[8,256,256]{2,1,0:T(8,128)} %all-reduce.2.cloned.1.call-done), kind=kLoop, calls=%fused_computation.39 | loop fusion | flops 524288 | bytes 4194304 | tf_op jit(solution)/shard_map/mul | solution.py:89
  194.8 0.0 reduce-scatter.2.cloned.1.call-done
  194.8 3.2 %convert_element_type.103 = bf16[3072,256]{1,0:T(8,128)(2,1)} convert(f32[3072,256]{1,0:T(8,128)} %reduce-scatter.2.cloned.1.call-done) | non-fusion elementwise | flops 786432 | bytes 4718592 | tf_op jit(solution)/shard_map/convert_element_type | solution.py:105
  (11 shorter events, 0.1 us)
Async XLA Ops:
  8.0 15.3 %copy-start = (bf16[6144,256]{1,0:T(8,128)(2,1)S(1)}, bf16[6144,256]{1,0:T(8,128)(2,1)}, u32[]{:S(2)}) copy-start(bf16[6144,256]{1,0:T(8,128)(2,1)} %param.8) | copy-start | bytes 9437188
  9.5 13.5 %all-to-all-start = ((s32[16,1,8]{2,1,0:T(1,128)}), s32[16,1,8]{2,1,0:T(1,128)S(1)}, u32[]{:S(2)}, u32[]{:S(2)}) async-start(s32[16,1,8]{2,1,0:T(1,128)} %copy.21), calls=%async_computation | async-start | bytes 16384 | tf_op jit(solution)/shard_map/all_to_all | solution.py:45
  24.9 11.5 %all-to-all-start.1 = ((bf16[16,8,256]{2,1,0:T(8,128)(2,1)}), bf16[16,8,256]{2,1,0:T(8,128)(2,1)S(1)}, u32[]{:S(2)}, u32[]{:S(2)}) async-start(bf16[16,8,256]{2,1,0:T(8,128)(2,1)} %bitcast_select_fusion), calls=%async_computation.1 | async-start | bytes 131072 | tf_op jit(solution)/shard_map/all_to_all | solution.py:47
  29.9 161.7 %all-reduce.2.cloned.1.call-start = ((), (), s32[]{:S(2)}) async-start(), calls=%async_computation.5 | async-start | bytes 4194304 | tf_op jit(solution)/shard_map/psum | solution.py:86
  39.4 1.3 copy-start.3
  40.7 2.0 copy-start.4
  57.0 2.6 %copy-start.1 = (f32[1024,256]{1,0:T(8,128)S(1)}, f32[1024,256]{1,0:T(8,128)}, u32[]{:S(2)}) copy-start(f32[1024,256]{1,0:T(8,128)} %fusion.48) | copy-start | bytes 3145732
  57.0 2.6 %copy-start.2 = (f32[1024,256]{1,0:T(8,128)S(1)}, f32[1024,256]{1,0:T(8,128)}, u32[]{:S(2)}) copy-start(f32[1024,256]{1,0:T(8,128)} %convert_multiply_fusion.2) | copy-start | bytes 3145732
  62.4 12.7 %all-to-all-start.2 = ((f32[16,8,256]{2,1,0:T(8,128)}), f32[16,8,256]{2,1,0:T(8,128)S(1)}, u32[]{:S(2)}, u32[]{:S(2)}) async-start(f32[16,8,256]{2,1,0:T(8,128)} %fusion.23), calls=%async_computation.2 | async-start | bytes 262144 | tf_op jit(solution)/shard_map/all_to_all | solution.py:92
  67.7 127.1 %reduce-scatter.2.cloned.1.call-start = ((), (), s32[]{:S(2)}) async-start(), calls=%async_computation.4 | async-start | bytes 9437184 | tf_op jit(solution)/shard_map/reduce_scatter | solution.py:104
Sparse Core Ops, SparseCore 0:
  57.1 134.5 all-reduce.1
Sparse Core Ops, SparseCore 1:
  79.4 14.7 reduce-scatter.1
where the time goes:
time: 208 us; the launch traced here: 205 us
  waiting for transfers between devices  121 us (58%)
  matrix products  22.5 us (11%)
  between operations  19.8 us (10%)
  other arithmetic  19 us (9%)
  starting transfers between devices  17.8 us (9%)
  local copies, waits for them, and re-layouts  5.52 us (3%)
    psum x1, waiting for transfers between devices, shards(): operator_total = lax.psum(operator_acc, ('rows', 'rep'))  112 us
    all_to_all x1, starting transfers between devices, shards(): lax.all_to_all(requests, 'rows', split_axis=0, concat_axis=0, tiled=True)  7.41 us
    all_to_all x1, waiting for transfers between devices, shards(): lax.all_to_all(slot_grad.reshape(owner_count, capacity, row_width), 'rows...  6 us
    all_to_all x1, starting transfers between devices, shards(): lax.all_to_all(slot_grad.reshape(owner_count, capacity, row_width), 'rows...  5.31 us
    all_to_all x1, starting transfers between devices, shards(): lax.all_to_all(serve_picked, 'rows', split_axis=0, concat_axis=0, tiled=T...  5.02 us
    scatter-add x1, other arithmetic, shards(): jnp.zeros((entity_table.shape[0], row_width), jnp.float32).at[flat_index]  4.29 us
  transfers between devices with their start and end apart: 5, of which 4 were waited for; matrix products, arithmetic and copies ran while one was open for 10% of the time, Pallas kernels for 0%

commit v1 on v0

v1 whole, which is shorter than its diff:
```python
import functools

import jax
import jax.numpy as jnp
from jax import lax
from jax.experimental import pallas as pl
from jax.experimental.pallas import tpu as pltpu
from jax.sharding import PartitionSpec as P

LANES = 128
TILE = 8
REL_LANE = 16
CID_LANE = 64


def pack(rows):
    cubes = rows.reshape(rows.shape[0] // TILE, TILE, rows.shape[1])
    return jnp.concatenate([cubes[:, :, :LANES], cubes[:, :, LANES:]], axis=1).astype(jnp.bfloat16)


def unpack(packed):
    wide = packed.astype(jnp.float32)
    joined = jnp.concatenate([wide[:, :TILE, :], wide[:, TILE:, :]], axis=2)
    return joined.reshape(joined.shape[0] * TILE, joined.shape[2])


def column(messages, first_lane):
    count = messages.shape[0]
    wide = jnp.broadcast_to(messages.astype(jnp.float32), (count, TILE, LANES)).reshape(count * TILE, LANES)
    lane = lax.broadcasted_iota(jnp.int32, wide.shape, 1)
    row = lax.rem(lax.broadcasted_iota(jnp.int32, wide.shape, 0), TILE)
    return jnp.sum(jnp.where(lane == row + first_lane, wide, 0.0), axis=1, keepdims=True)


def dot(left, right, left_dim, right_dim):
    return lax.dot_general(
        left, right, (((left_dim,), (right_dim,)), ((), ())), preferred_element_type=jnp.float32
    )


def split(value):
    upper = value.astype(jnp.bfloat16)
    return upper, (value - upper.astype(jnp.float32)).astype(jnp.bfloat16)


def kernel(
    n_rows, n_rep, scale,
    relation_ref, head_ref, source_ref, target_ref, negative_ref, table_hbm, ops_hbm,
    entity_ref, relation_out,
    table, operators, requests, served, slots_in, grad_out, grad_in, op_out, op_in, relation_of, gathered,
    pair_count, negative_count, row_acc,
    local_sem, send_sem, receive_sem, gather_sem, fan_sem, pass_sem,
):
    devices = n_rows * n_rep
    my_row, my_rep = lax.axis_index("rows"), lax.axis_index("rep")
    me = my_row * n_rep + my_rep
    my_slot = my_rep * n_rows + my_row
    other_rep = n_rep - 1 - my_rep
    blocks = source_ref.shape[0]
    relations, width, _ = operators.shape
    reducers = width // TILE
    stride = devices // reducers
    weight_neg = negative_ref.shape[1] ** (-0.5)

    table_copy = pltpu.make_async_copy(table_hbm, table, local_sem.at[0])
    table_copy.start()
    ops_copy = pltpu.make_async_copy(ops_hbm, operators, local_sem.at[1])
    ops_copy.start()

    def remote(source, destination, send, receive, row, rep):
        return pltpu.make_async_remote_copy(
            src_ref=source, dst_ref=destination, send_sem=send, recv_sem=receive,
            device_id=(row, rep), device_id_type=pl.DeviceIdType.MESH,
        )

    def settle(buffer, semaphore):
        pltpu.make_async_copy(buffer, buffer, semaphore).wait()

    barrier = pltpu.get_barrier_semaphore()

    @pl.loop(1, devices)
    def _(step):
        other = lax.rem(me + step, devices)
        pl.semaphore_signal(
            barrier, inc=1, device_id=(lax.div(other, n_rep), lax.rem(other, n_rep)),
            device_id_type=pl.DeviceIdType.MESH,
        )

    pl.semaphore_wait(barrier, devices - 1)

    own_request = pltpu.make_async_copy(head_ref.at[my_row], requests.at[my_slot], receive_sem.at[0])
    own_request.start()

    @pl.loop(1, n_rows)
    def _(step):
        row = lax.rem(my_row + step, n_rows)
        remote(head_ref.at[row], requests.at[my_slot], send_sem.at[0], receive_sem.at[0], row, my_rep).start()

    @pl.loop(0, n_rows)
    def _(step):
        row = lax.rem(my_row + step, n_rows)
        remote(head_ref.at[row], requests.at[my_slot], send_sem.at[1], receive_sem.at[1], row, other_rep).start()

    compact = column(head_ref[...], CID_LANE).astype(jnp.int32)
    for block in range(blocks):
        hit = [
            (compact == ids[block : block + 1, :]).astype(jnp.float32).astype(jnp.bfloat16)
            for ids in (source_ref, target_ref, negative_ref)
        ]
        pair_count[block] = dot(hit[0], hit[1], 1, 1)
        ones = jnp.ones((TILE, hit[2].shape[1]), jnp.bfloat16)
        negative_count[block] = dot(ones, hit[2], 1, 1)

    settle(requests.at[pl.ds(my_rep * n_rows, n_rows)], receive_sem.at[0])
    wanted = column(requests[pl.ds(my_rep * n_rows, n_rows)], 0).astype(jnp.int32)
    table_copy.wait()
    step_rows = 512
    row_acc[...] = jnp.zeros_like(row_acc)

    @pl.loop(0, table.shape[0] // step_rows)
    def _(step):
        first = pl.multiple_of(step * step_rows, step_rows)
        lane = lax.broadcasted_iota(jnp.int32, (wanted.shape[0], step_rows), 1) + first
        pick = (wanted == lane).astype(jnp.float32).astype(jnp.bfloat16)
        row_acc[...] += dot(pick, table[pl.ds(first, step_rows), :], 1, 0)

    served[...] = pack(row_acc[...])
    own_rows = pltpu.make_async_copy(served.at[my_row], slots_in.at[my_row], receive_sem.at[2])
    own_rows.start()

    @pl.loop(1, n_rows)
    def _(step):
        row = lax.rem(my_row + step, n_rows)
        remote(served.at[row], slots_in.at[my_row], send_sem.at[2], receive_sem.at[2], row, my_rep).start()

    settle(requests.at[pl.ds(other_rep * n_rows, n_rows)], receive_sem.at[1])
    heads = requests[...].astype(jnp.float32)
    head_lane = lax.broadcasted_iota(jnp.int32, heads.shape, 2)
    for block in range(blocks):
        kind = jnp.sum(jnp.where(head_lane == REL_LANE + block, heads, 0.0), axis=2, keepdims=True)
        relation_of[block] = jnp.broadcast_to(kind, heads.shape)
    ops_copy.wait()
    settle(slots_in, receive_sem.at[2])

    slots = unpack(slots_in[...]).astype(jnp.bfloat16)
    slot_grad = jnp.zeros(slots.shape, jnp.float32)
    for block in range(blocks):
        operator = operators[relation_ref[block]]
        query = dot(slots, operator, 1, 0).astype(jnp.bfloat16)
        scores = dot(query, slots, 1, 1)
        pairs = pair_count[block]
        source_count = jnp.sum(pairs, axis=1, keepdims=True)
        coefficient = source_count * negative_count[block][:1, :] * (jax.nn.sigmoid(scores) * weight_neg)
        coefficient = coefficient - pairs * jax.nn.sigmoid(-scores)
        upper, lower = split(coefficient)
        query_grad = (dot(upper, slots, 1, 0) + dot(lower, slots, 1, 0)).astype(jnp.bfloat16)
        op_out[:, block] = pack(dot(slots, query_grad, 0, 0))
        slot_grad = slot_grad + dot(query_grad, operator, 1, 1)
        slot_grad = slot_grad + dot(upper, query, 0, 0) + dot(lower, query, 0, 0)
    grad_out[...] = pack(slot_grad)

    my_reducer = lax.div(me, stride)
    reducing = lax.rem(me, stride) == 0

    @pl.loop(0, reducers)
    def _(step):
        reducer = lax.rem(my_reducer + 1 + step, reducers)
        device = reducer * stride

        @pl.when(device != me)
        def _():
            remote(
                op_out.at[reducer], op_in.at[my_slot], send_sem.at[3], receive_sem.at[3],
                lax.div(device, n_rep), lax.rem(device, n_rep),
            ).start()

        @pl.when(device == me)
        def _():
            pltpu.make_async_copy(op_out.at[reducer], op_in.at[my_slot], receive_sem.at[3]).start()

    pltpu.make_async_copy(grad_out.at[my_row], grad_in.at[my_slot], receive_sem.at[4]).start()

    @pl.loop(1, devices)
    def _(step):
        device = lax.rem(me + step, devices)
        row = lax.div(device, n_rep)
        remote(
            grad_out.at[row], grad_in.at[my_slot], send_sem.at[4], receive_sem.at[4], row, lax.rem(device, n_rep)
        ).start()

    @pl.when(reducing)
    def _():
        settle(op_in, receive_sem.at[3])

        def add(source, totals):
            totals = list(totals)
            for block in range(blocks):
                term = op_in[source, block].astype(jnp.float32)
                kind = relation_of[block, source]
                for relation in range(relations):
                    totals[relation] = totals[relation] + jnp.where(kind == float(relation), term, 0.0)
            return tuple(totals)

        zero = jnp.zeros(op_in.shape[2:], jnp.float32)
        totals = lax.fori_loop(0, devices, add, (zero,) * relations)
        for relation in range(relations):
            gathered[my_reducer, relation] = (totals[relation] * scale).astype(jnp.bfloat16)

        piece = gathered.at[my_reducer]

        @pl.loop(1, n_rows)
        def _(step):
            row = lax.rem(my_row + step, n_rows)
            remote(piece, piece, fan_sem.at[row], gather_sem.at[my_reducer], row, my_rep).start()

        remote(piece, piece, fan_sem.at[my_row], gather_sem.at[my_reducer], my_row, other_rep).start()

    settle(grad_in, receive_sem.at[4])
    all_rows = column(requests[...], 0).astype(jnp.int32)
    grads = unpack(grad_in[...]).astype(jnp.bfloat16)
    half = entity_ref.shape[0]

    @pl.loop(0, half // step_rows)
    def _(step):
        first = pl.multiple_of(step * step_rows, step_rows)
        lane = lax.broadcasted_iota(jnp.int32, (all_rows.shape[0], step_rows), 1) + first + my_rep * half
        place = (all_rows == lane).astype(jnp.float32).astype(jnp.bfloat16)
        entity_ref[pl.ds(first, step_rows), :] = dot(place, grads, 0, 0).astype(jnp.bfloat16)

    def spread(reducer):
        rows = gathered[reducer].astype(jnp.float32)
        first = pl.multiple_of(reducer * TILE, TILE)
        relation_out[:, pl.ds(first, TILE), :] = jnp.concatenate([rows[:, :TILE, :], rows[:, TILE:, :]], axis=2)

    @pl.loop(0, reducers)
    def _(step):
        reducer = lax.rem(my_reducer + reducers - step, reducers)
        device = reducer * stride
        piece = gathered.at[reducer]

        @pl.when(lax.rem(device, n_rep) == my_rep)
        def _():
            @pl.when(device != me)
            def _():
                settle(piece, gather_sem.at[reducer])
                remote(piece, piece, pass_sem.at[reducer], gather_sem.at[reducer], my_row, other_rep).start()

            spread(reducer)

    @pl.loop(0, reducers)
    def _(step):
        reducer = lax.rem(my_reducer + reducers - step, reducers)

        @pl.when(lax.rem(reducer * stride, n_rep) != my_rep)
        def _():
            settle(gathered.at[reducer], gather_sem.at[reducer])
            spread(reducer)

    settle(head_ref.at[pl.ds(0, n_rows - 1)], send_sem.at[0])
    settle(head_ref, send_sem.at[1])
    settle(served.at[pl.ds(0, n_rows - 1)], send_sem.at[2])
    settle(op_out.at[pl.ds(0, reducers - 1)], send_sem.at[3])

    @pl.when(jnp.logical_not(reducing))
    def _():
        settle(op_out.at[0], send_sem.at[3])

    settle(grad_in.at[pl.ds(0, devices - 1)], send_sem.at[4])

    @pl.when(reducing)
    def _():
        @pl.loop(0, n_rows)
        def _(row):
            settle(gathered.at[my_reducer], fan_sem.at[row])

    @pl.loop(0, reducers)
    def _(reducer):
        device = reducer * stride

        @pl.when(jnp.logical_and(lax.rem(device, n_rep) == my_rep, device != me))
        def _():
            settle(gathered.at[reducer], pass_sem.at[reducer])


def shards(
    entity_table, relation_ops, need_rows, send_offsets, source_ids, target_ids, negative_ids, relation_ids
):
    n_rows, n_rep = lax.axis_size("rows"), lax.axis_size("rep")
    devices = n_rows * n_rep
    need = need_rows[0, 0]
    capacity = need.shape[1]
    offsets = send_offsets[0, 0]
    blocks, edges = source_ids.shape[2:]
    relations, width, _ = relation_ops.shape
    reducers = width // TILE
    slot_lane = jnp.arange(capacity, dtype=jnp.int32)[None, :]
    compact = offsets[:-1, None] + slot_lane
    compact = jnp.where(compact < offsets[1:, None], compact, -1)
    kinds = jnp.broadcast_to(relation_ids[0, 0][None, :], (n_rows, blocks))
    head = (
        jnp.pad(need, ((0, 0), (0, LANES - capacity)))
        + jnp.pad(kinds, ((0, 0), (REL_LANE, LANES - REL_LANE - blocks)))
        + jnp.pad(compact, ((0, 0), (CID_LANE, LANES - CID_LANE - capacity)))
    ).reshape(n_rows, 1, LANES)
    scale = (relations / (edges * blocks * devices)) ** 0.5
    packed = (2 * TILE, LANES)
    slots = n_rows * capacity
    vmem = pl.BlockSpec(memory_space=pltpu.VMEM)
    anywhere = pl.BlockSpec(memory_space=pl.ANY)
    return pl.pallas_call(
        functools.partial(kernel, n_rows, n_rep, scale),
        out_shape=(
            jax.ShapeDtypeStruct((entity_table.shape[0] // n_rep, width), jnp.bfloat16),
            jax.ShapeDtypeStruct(relation_ops.shape, jnp.float32),
        ),
        in_specs=[pl.BlockSpec(memory_space=pltpu.SMEM), vmem, vmem, vmem, vmem, anywhere, anywhere],
        out_specs=(vmem, vmem),
        scratch_shapes=[
            pltpu.VMEM(entity_table.shape, jnp.bfloat16),
            pltpu.VMEM(relation_ops.shape, jnp.bfloat16),
            pltpu.VMEM((devices, 1, LANES), jnp.int32),
            pltpu.VMEM((n_rows, *packed), jnp.bfloat16),
            pltpu.VMEM((n_rows, *packed), jnp.bfloat16),
            pltpu.VMEM((n_rows, *packed), jnp.bfloat16),
            pltpu.VMEM((devices, *packed), jnp.bfloat16),
            pltpu.VMEM((reducers, blocks, *packed), jnp.bfloat16),
            pltpu.VMEM((devices, blocks, *packed), jnp.bfloat16),
            pltpu.VMEM((blocks, devices, 1, LANES), jnp.float32),
            pltpu.VMEM((reducers, relations, *packed), jnp.bfloat16),
            pltpu.VMEM((blocks, slots, slots), jnp.float32),
            pltpu.VMEM((blocks, TILE, slots), jnp.float32),
            pltpu.VMEM((slots, width), jnp.float32),
            pltpu.SemaphoreType.DMA((2,)),
            pltpu.SemaphoreType.DMA((5,)),
            pltpu.SemaphoreType.DMA((5,)),
            pltpu.SemaphoreType.DMA((reducers,)),
            pltpu.SemaphoreType.DMA((n_rows,)),
            pltpu.SemaphoreType.DMA((reducers,)),
        ],
        compiler_params=pltpu.CompilerParams(
            collective_id=0, has_side_effects=True, vmem_limit_bytes=52 * 1024 * 1024
        ),
    )(
        relation_ids[0, 0], head, source_ids[0, 0], target_ids[0, 0], negative_ids[0, 0],
        entity_table, relation_ops,
    )


def solution(mesh):
    return jax.shard_map(
        shards,
        mesh=mesh,
        in_specs=(
            P("rows", None),
            P(),
            P("rows", "rep", None, None),
            P("rows", "rep", None),
            P("rows", "rep", None, None),
            P("rows", "rep", None, None),
            P("rows", "rep", None, None),
            P("rows", "rep", None),
        ),
        out_specs=(P(("rows", "rep"), None), P()),
        check_vma=False,
    )
```

time: 208 us -> 55.8 us (0.27)
  the two profiles are of different devices: /device:TPU:1 before, /device:TPU:29 now
where the time goes in v1:
time: 55.8 us; the launch traced here: 55.4 us
  Pallas kernels  44.2 us (79%)
  local copies, waits for them, and re-layouts  10.4 us (19%)
  between operations  0.65 us (1%)
    pallas_call x1, Pallas kernels, shards(): pl.pallas_call(functools.partial(kernel, n_rows, n_rep, scale), out_shape...  44.2 us
    unnamed x14, local copies, waits for them, and re-layouts  8.09 us

profile of v1, /device:TPU:29, one launch (start us, length us, event | category | flops | bytes accessed | tf_op | source)
XLA Modules:
  0.0 55.4 jit_solution(2927314745734204142)
XLA Ops:
  0.6 0.7 %pad.15 = s32[128]{0:T(128)S(1)} pad(s32[2]{0:T(128)} %bitcast.14, s32[]{:T(128)} %constant.0.clone.1), padding=16_110 | pad | bytes 524 | tf_op jit(solution)/shard_map/jit(_pad)/pad | solution.py:302
  1.4 0.8 %slice_bitcast_fusion.1 = (s32[16]{0:T(128)S(1)}, s32[16]{0:T(128)S(1)}) fusion(s32[1,1,17]{2,1,0:T(1,128)} %param.11), kind=kLoop, calls=%fused_computation.3 | loop fusion | bytes 256 | tf_op jit(solution)/shard_map/add | solution.py:297
  2.2 0.1 compare_select_fusion
  2.2 0.8 %copy.10 = s32[16,8]{1,0:T(8,128)S(1)} copy(s32[16,8]{0,1:T(8,128)} %bitcast.16) | data formatting | bytes 1024 | tf_op jit(solution)/shard_map/squeeze | solution.py:290
  3.0 0.1 pad_add_fusion
  3.1 0.0 copy-start
  3.1 1.2 %copy-done = bf16[8,256,256]{2,1,0:T(8,128)(2,1)S(1)} copy-done((bf16[8,256,256]{2,1,0:T(8,128)(2,1)S(1)}, bf16[8,256,256]{2,1,0:T(8,128)(2,1)}, u32[]{:S(2)}) %copy-start) | copy-done | bytes 1048600
  4.3 0.0 copy-start.1
  4.3 0.7 %copy-done.1 = s32[1,1,2,1024]{3,2,1,0:T(2,128)S(1)} copy-done((s32[1,1,2,1024]{3,2,1,0:T(2,128)S(1)}, s32[1,1,2,1024]{3,2,1,0:T(2,128)}, u32[]{:S(2)}) %copy-start.1) | copy-done | bytes 8216
  5.0 0.0 copy-start.2
  5.0 0.7 %copy-done.2 = s32[1,1,2,1024]{3,2,1,0:T(2,128)S(1)} copy-done((s32[1,1,2,1024]{3,2,1,0:T(2,128)S(1)}, s32[1,1,2,1024]{3,2,1,0:T(2,128)}, u32[]{:S(2)}) %copy-start.2) | copy-done | bytes 8216
  5.7 0.0 copy-start.3
  5.7 0.7 %copy-done.3 = s32[1,1,2,1024]{3,2,1,0:T(2,128)S(1)} copy-done((s32[1,1,2,1024]{3,2,1,0:T(2,128)S(1)}, s32[1,1,2,1024]{3,2,1,0:T(2,128)}, u32[]{:S(2)}) %copy-start.3) | copy-done | bytes 8216
  6.4 0.0 copy-start.4
  6.4 0.7 %copy-done.4 = s32[1,1,2]{2,1,0:T(1,128)S(1)} copy-done((s32[1,1,2]{2,1,0:T(1,128)S(1)}, s32[1,1,2]{2,1,0:T(1,128)}, u32[]{:S(2)}) %copy-start.4) | copy-done | bytes 32
  7.0 44.2 %shard_map.95 = (bf16[3072,256]{1,0:T(8,128)(2,1)}, f32[8,256,256]{2,1,0:T(8,128)}) custom-call(s32[2]{0:T(128)S(1)} %bitcast.15, s32[16,1,128]{2,1,0:T(1,128)S(1)} %bitcast.10, s32[2,1024]{1,0:T(2,128)S(1)} %bitcast.11, s32[2,1024]{1,0:T(2,128)S(1)} %bitcast.12, s32[2,1024]{1,0:T(2,128)S(1)} %bitcast.13, bf16[6144,256]{1,0:T(8,128)(2,1)} %table_hbm.1, ...), custom_call_target="tpu_custom_call" | custom-call | tf_op jit(solution)/shard_map/pallas_call | solution.py:310
  51.3 0.0 copy-start.5
  51.3 2.8 %copy.13 = bf16[3072,256]{1,0:T(8,128)(2,1)} copy(bf16[3072,256]{1,0:T(8,128)(2,1)} %get-tuple-element.6) | data formatting | bytes 3145728
  54.1 0.0 copy-done.5
  54.1 1.3 %copy.14 = f32[8,256,256]{2,1,0:T(8,128)} copy(f32[8,256,256]{2,1,0:T(8,128)S(1)} %copy-done.5) | data formatting | bytes 4194304
Async XLA Ops:
  3.1 1.2 %copy-start = (bf16[8,256,256]{2,1,0:T(8,128)(2,1)S(1)}, bf16[8,256,256]{2,1,0:T(8,128)(2,1)}, u32[]{:S(2)}) copy-start(bf16[8,256,256]{2,1,0:T(8,128)(2,1)} %ops_hbm.1) | copy-start | bytes 3145732
  4.3 0.7 %copy-start.1 = (s32[1,1,2,1024]{3,2,1,0:T(2,128)S(1)}, s32[1,1,2,1024]{3,2,1,0:T(2,128)}, u32[]{:S(2)}) copy-start(s32[1,1,2,1024]{3,2,1,0:T(2,128)} %param.12) | copy-start | bytes 24580
  5.0 0.7 %copy-start.2 = (s32[1,1,2,1024]{3,2,1,0:T(2,128)S(1)}, s32[1,1,2,1024]{3,2,1,0:T(2,128)}, u32[]{:S(2)}) copy-start(s32[1,1,2,1024]{3,2,1,0:T(2,128)} %param.13) | copy-start | bytes 24580
  5.7 0.7 %copy-start.3 = (s32[1,1,2,1024]{3,2,1,0:T(2,128)S(1)}, s32[1,1,2,1024]{3,2,1,0:T(2,128)}, u32[]{:S(2)}) copy-start(s32[1,1,2,1024]{3,2,1,0:T(2,128)} %param.14) | copy-start | bytes 24580
  6.4 0.7 %copy-start.4 = (s32[1,1,2]{2,1,0:T(1,128)S(1)}, s32[1,1,2]{2,1,0:T(1,128)}, u32[]{:S(2)}) copy-start(s32[1,1,2]{2,1,0:T(1,128)} %param.15) | copy-start | bytes 28
  51.3 2.8 %copy-start.5 = (f32[8,256,256]{2,1,0:T(8,128)S(1)}, f32[8,256,256]{2,1,0:T(8,128)}, u32[]{:S(2)}) copy-start(f32[8,256,256]{2,1,0:T(8,128)} %get-tuple-element.7) | copy-start | bytes 6291460

commit v2 on v1

--- a/solution.py
+++ b/solution.py
@@ -10,7 +10,7 @@
 LANES = 128
 TILE = 8
 REL_LANE = 16
-CID_LANE = 64
+PLANE = 4
 
 
 def pack(rows):
@@ -45,8 +45,9 @@
 
 def kernel(
     n_rows, n_rep, scale,
-    relation_ref, head_ref, source_ref, target_ref, negative_ref, table_hbm, ops_hbm,
-    entity_ref, relation_out,
+    relation_ref, offset_ref, need_hbm, source_hbm, target_hbm, negative_hbm, table_hbm, ops_hbm,
+    entity_hbm, relation_out,
+    need_ref, source_ref, target_ref, negative_ref, head_ref, compact_ref, entity_ref,
     table, operators, requests, served, slots_in, grad_out, grad_in, op_out, op_in, relation_of, gathered,
     pair_count, negative_count, row_acc,
     local_sem, send_sem, receive_sem, gather_sem, fan_sem, pass_sem,
@@ -66,6 +67,16 @@
     table_copy.start()
     ops_copy = pltpu.make_async_copy(ops_hbm, operators, local_sem.at[1])
     ops_copy.start()
+    need_copy = pltpu.make_async_copy(need_hbm, need_ref, local_sem.at[2])
+    need_copy.start()
+    id_copies = [
+        pltpu.make_async_copy(hbm, ref, local_sem.at[3 + index])
+        for index, (hbm, ref) in enumerate(
+            ((source_hbm, source_ref), (target_hbm, target_ref), (negative_hbm, negative_ref))
+        )
+    ]
+    for id_copy in id_copies:
+        id_copy.start()
 
     def remote(source, destination, send, receive, row, rep):
         return pltpu.make_async_remote_copy(
@@ -86,6 +97,20 @@
             device_id_type=pl.DeviceIdType.MESH,
         )
 
+    lane = lax.broadcasted_iota(jnp.int32, (TILE, LANES), 1)
+    sublane = lax.broadcasted_iota(jnp.int32, (TILE, LANES), 0)
+    kinds = jnp.zeros((1, LANES), jnp.int32)
+    for block in range(blocks):
+        kinds = jnp.where(lane[:1] == REL_LANE + block, relation_ref[block], kinds)
+    need_copy.wait()
+    need = need_ref[...].astype(jnp.float32)
+    for row in range(n_rows):
+        wide = jnp.where(lane == sublane, jnp.broadcast_to(need[:, row : row + 1], lane.shape), 0.0)
+        head_ref[row] = jnp.sum(wide, axis=0, keepdims=True).astype(jnp.int32) + kinds
+        first_id = offset_ref[row]
+        slot_id = first_id + sublane
+        compact_ref[row * TILE : (row + 1) * TILE, :] = jnp.where(slot_id < offset_ref[row + 1], slot_id, -1)
+
     pl.semaphore_wait(barrier, devices - 1)
 
     own_request = pltpu.make_async_copy(head_ref.at[my_row], requests.at[my_slot], receive_sem.at[0])
@@ -101,7 +126,9 @@
         row = lax.rem(my_row + step, n_rows)
         remote(head_ref.at[row], requests.at[my_slot], send_sem.at[1], receive_sem.at[1], row, other_rep).start()
 
-    compact = column(head_ref[...], CID_LANE).astype(jnp.int32)
+    for id_copy in id_copies:
+        id_copy.wait()
+    compact = compact_ref[:, :1]
     for block in range(blocks):
         hit = [
             (compact == ids[block : block + 1, :]).astype(jnp.float32).astype(jnp.bfloat16)
@@ -208,12 +235,16 @@
 
         piece = gathered.at[my_reducer]
 
-        @pl.loop(1, n_rows)
+        @pl.loop(1, n_rows // PLANE)
         def _(step):
-            row = lax.rem(my_row + step, n_rows)
-            remote(piece, piece, fan_sem.at[row], gather_sem.at[my_reducer], row, my_rep).start()
-
-        remote(piece, piece, fan_sem.at[my_row], gather_sem.at[my_reducer], my_row, other_rep).start()
+            row = lax.rem(my_row + step * PLANE, n_rows)
+            remote(piece, piece, fan_sem.at[PLANE + step], gather_sem.at[my_reducer], row, my_rep).start()
+
+        for step in range(1, PLANE):
+            row = lax.div(my_row, PLANE) * PLANE + lax.rem(my_row + step, PLANE)
+            remote(piece, piece, fan_sem.at[step], gather_sem.at[my_reducer], row, my_rep).start()
+
+        remote(piece, piece, fan_sem.at[0], gather_sem.at[my_reducer], my_row, other_rep).start()
 
     settle(grad_in, receive_sem.at[4])
     all_rows = column(requests[...], 0).astype(jnp.int32)
@@ -227,34 +258,53 @@
         place = (all_rows == lane).astype(jnp.float32).astype(jnp.bfloat16)
         entity_ref[pl.ds(first, step_rows), :] = dot(place, grads, 0, 0).astype(jnp.bfloat16)
 
-    def spread(reducer):
-        rows = gathered[reducer].astype(jnp.float32)
-        first = pl.multiple_of(reducer * TILE, TILE)
-        relation_out[:, pl.ds(first, TILE), :] = jnp.concatenate([rows[:, :TILE, :], rows[:, TILE:, :]], axis=2)
+    entity_copy = pltpu.make_async_copy(entity_ref, entity_hbm, local_sem.at[6])
+    entity_copy.start()
+
+    def mine(reducer):
+        device = reducer * stride
+        same_rep = lax.rem(device, n_rep) == my_rep
+        same_column = lax.rem(lax.div(device, n_rep), PLANE) == lax.rem(my_row, PLANE)
+        first = jnp.logical_and(jnp.logical_and(same_rep, same_column), device != me)
+        second = jnp.logical_and(same_rep, jnp.logical_not(same_column))
+        return first, second
 
     @pl.loop(0, reducers)
     def _(step):
-        reducer = lax.rem(my_reducer + reducers - step, reducers)
-        device = reducer * stride
+        reducer = lax.rem(my_reducer + 1 + step, reducers)
         piece = gathered.at[reducer]
 
-        @pl.when(lax.rem(device, n_rep) == my_rep)
-        def _():
-            @pl.when(device != me)
+        @pl.when(mine(reducer)[0])
+        def _():
+            settle(piece, gather_sem.at[reducer])
+            for hop in range(1, PLANE):
+                row = lax.div(my_row, PLANE) * PLANE + lax.rem(my_row + hop, PLANE)
+                remote(piece, piece, pass_sem.at[reducer, hop], gather_sem.at[reducer], row, my_rep).start()
+            remote(piece, piece, pass_sem.at[reducer, 0], gather_sem.at[reducer], my_row, other_rep).start()
+
+    @pl.loop(0, reducers)
+    def _(step):
+        reducer = lax.rem(my_reducer + 1 + step, reducers)
+        piece = gathered.at[reducer]
+
+        @pl.when(mine(reducer)[1])
+        def _():
+            settle(piece, gather_sem.at[reducer])
+            remote(piece, piece, pass_sem.at[reducer, 0], gather_sem.at[reducer], my_row, other_rep).start()
+
+    @pl.loop(0, reducers // 2)
+    def _(pair):
+        halves = []
+        for reducer in (2 * pair, 2 * pair + 1):
+
+            @pl.when(lax.rem(reducer * stride, n_rep) != my_rep)
             def _():
-                settle(piece, gather_sem.at[reducer])
-                remote(piece, piece, pass_sem.at[reducer], gather_sem.at[reducer], my_row, other_rep).start()
-
-            spread(reducer)
-
-    @pl.loop(0, reducers)
-    def _(step):
-        reducer = lax.rem(my_reducer + reducers - step, reducers)
-
-        @pl.when(lax.rem(reducer * stride, n_rep) != my_rep)
-        def _():
-            settle(gathered.at[reducer], gather_sem.at[reducer])
-            spread(reducer)
+                settle(gathered.at[reducer], gather_sem.at[reducer])
+
+            rows = gathered[reducer].astype(jnp.float32)
+            halves.append(jnp.concatenate([rows[:, :TILE, :], rows[:, TILE:, :]], axis=2))
+        first = pl.multiple_of(pair * 2 * TILE, 2 * TILE)
+        relation_out[:, pl.ds(first, 2 * TILE), :] = jnp.concatenate(halves, axis=1).astype(jnp.bfloat16)
 
     settle(head_ref.at[pl.ds(0, n_rows - 1)], send_sem.at[0])
     settle(head_ref, send_sem.at[1])
@@ -269,17 +319,27 @@
 
     @pl.when(reducing)
     def _():
-        @pl.loop(0, n_rows)
-        def _(row):
-            settle(gathered.at[my_reducer], fan_sem.at[row])
+        for step in range(PLANE):
+            settle(gathered.at[my_reducer], fan_sem.at[step])
+
+        @pl.loop(1, n_rows // PLANE)
+        def _(step):
+            settle(gathered.at[my_reducer], fan_sem.at[PLANE + step])
 
     @pl.loop(0, reducers)
     def _(reducer):
-        device = reducer * stride
-
-        @pl.when(jnp.logical_and(lax.rem(device, n_rep) == my_rep, device != me))
-        def _():
-            settle(gathered.at[reducer], pass_sem.at[reducer])
+        first, second = mine(reducer)
+
+        @pl.when(jnp.logical_or(first, second))
+        def _():
+            settle(gathered.at[reducer], pass_sem.at[reducer, 0])
+
+        @pl.when(first)
+        def _():
+            for hop in range(1, PLANE):
+                settle(gathered.at[reducer], pass_sem.at[reducer, hop])
+
+    entity_copy.wait()
 
 
 def shards(
@@ -289,33 +349,31 @@
     devices = n_rows * n_rep
     need = need_rows[0, 0]
     capacity = need.shape[1]
-    offsets = send_offsets[0, 0]
     blocks, edges = source_ids.shape[2:]
     relations, width, _ = relation_ops.shape
     reducers = width // TILE
-    slot_lane = jnp.arange(capacity, dtype=jnp.int32)[None, :]
-    compact = offsets[:-1, None] + slot_lane
-    compact = jnp.where(compact < offsets[1:, None], compact, -1)
-    kinds = jnp.broadcast_to(relation_ids[0, 0][None, :], (n_rows, blocks))
-    head = (
-        jnp.pad(need, ((0, 0), (0, LANES - capacity)))
-        + jnp.pad(kinds, ((0, 0), (REL_LANE, LANES - REL_LANE - blocks)))
-        + jnp.pad(compact, ((0, 0), (CID_LANE, LANES - CID_LANE - capacity)))
-    ).reshape(n_rows, 1, LANES)
     scale = (relations / (edges * blocks * devices)) ** 0.5
     packed = (2 * TILE, LANES)
     slots = n_rows * capacity
-    vmem = pl.BlockSpec(memory_space=pltpu.VMEM)
-    anywhere = pl.BlockSpec(memory_space=pl.ANY)
-    return pl.pallas_call(
+    hbm = pl.BlockSpec(memory_space=pltpu.HBM)
+    smem = pl.BlockSpec(memory_space=pltpu.SMEM)
+    entity_shape = (entity_table.shape[0] // n_rep, width)
+    entity_grad, relation_grad = pl.pallas_call(
         functools.partial(kernel, n_rows, n_rep, scale),
         out_shape=(
-            jax.ShapeDtypeStruct((entity_table.shape[0] // n_rep, width), jnp.bfloat16),
-            jax.ShapeDtypeStruct(relation_ops.shape, jnp.float32),
+            jax.ShapeDtypeStruct(entity_shape, jnp.bfloat16),
+            jax.ShapeDtypeStruct(relation_ops.shape, jnp.bfloat16),
         ),
-        in_specs=[pl.BlockSpec(memory_space=pltpu.SMEM), vmem, vmem, vmem, vmem, anywhere, anywhere],
-        out_specs=(vmem, vmem),
+        in_specs=[smem, smem] + [hbm] * 6,
+        out_specs=(hbm, pl.BlockSpec(memory_space=pltpu.VMEM)),
         scratch_shapes=[
+            pltpu.VMEM((capacity, n_rows), jnp.int32),
+            pltpu.VMEM((blocks, edges), jnp.int32),
+            pltpu.VMEM((blocks, edges), jnp.int32),
+            pltpu.VMEM((blocks, negative_ids.shape[-1]), jnp.int32),
+            pltpu.VMEM((n_rows, 1, LANES), jnp.int32),
+            pltpu.VMEM((slots, LANES), jnp.int32),
+            pltpu.VMEM(entity_shape, jnp.bfloat16),
             pltpu.VMEM(entity_table.shape, jnp.bfloat16),
             pltpu.VMEM(relation_ops.shape, jnp.bfloat16),
             pltpu.VMEM((devices, 1, LANES), jnp.int32),
@@ -330,20 +388,21 @@
             pltpu.VMEM((blocks, slots, slots), jnp.float32),
             pltpu.VMEM((blocks, TILE, slots), jnp.float32),
             pltpu.VMEM((slots, width), jnp.float32),
-            pltpu.SemaphoreType.DMA((2,)),
+            pltpu.SemaphoreType.DMA((7,)),
             pltpu.SemaphoreType.DMA((5,)),
             pltpu.SemaphoreType.DMA((5,)),
             pltpu.SemaphoreType.DMA((reducers,)),
-            pltpu.SemaphoreType.DMA((n_rows,)),
-            pltpu.SemaphoreType.DMA((reducers,)),
+            pltpu.SemaphoreType.DMA((PLANE + n_rows // PLANE,)),
+            pltpu.SemaphoreType.DMA((reducers, PLANE)),
         ],
         compiler_params=pltpu.CompilerParams(
-            collective_id=0, has_side_effects=True, vmem_limit_bytes=52 * 1024 * 1024
+            collective_id=0, has_side_effects=True, vmem_limit_bytes=64 * 1024 * 1024 - 16384
         ),
     )(
-        relation_ids[0, 0], head, source_ids[0, 0], target_ids[0, 0], negative_ids[0, 0],
+        relation_ids[0, 0], send_offsets[0, 0], need.T, source_ids[0, 0], target_ids[0, 0], negative_ids[0, 0],
         entity_table, relation_ops,
     )
+    return entity_grad, relation_grad.astype(jnp.float32)
 
 
 def solution(mesh):

time: 55.8 us -> 46.8 us (0.84)
  the two profiles are of different devices: /device:TPU:29 before, /device:TPU:1 now
where the time goes in v2:
time: 46.8 us; the launch traced here: 46.6 us
  Pallas kernels  42 us (90%)
  other arithmetic  2.85 us (6%)
  local copies, waits for them, and re-layouts  1.15 us (2%)
  between operations  0.65 us (1%)
    pallas_call x1, Pallas kernels, shards(): pl.pallas_call(functools.partial(kernel, n_rows, n_rep, scale), out_shape...  42 us
    convert_element_type x1, other arithmetic, shards(): return (entity_grad, relation_grad.astype(jnp.float32))  2.85 us
    unnamed x3, local copies, waits for them, and re-layouts  1.15 us

profile of v2, /device:TPU:1, one launch (start us, length us, event | category | flops | bytes accessed | tf_op | source)
XLA Modules:
  0.0 46.6 jit_solution(14558849872207301304)
XLA Ops:
  0.6 42.0 %shard_map.95 = (bf16[3072,256]{1,0:T(8,128)(2,1)}, bf16[8,256,256]{2,1,0:T(8,128)(2,1)}) custom-call(s32[2]{0:T(128)} %bitcast.12, s32[17]{0:T(128)} %bitcast.13, s32[8,16]{1,0:T(8,128)} %bitcast.11, s32[2,1024]{1,0:T(2,128)} %bitcast.8, s32[2,1024]{1,0:T(2,128)} %bitcast.9, s32[2,1024]{1,0:T(2,128)} %bitcast.10, bf16[6144,256]{1,0:T(8,128)(2,1)} %table_hbm.1, ...), custom_call_target="tpu_custom_call" | custom-call | tf_op jit(solution)/shard_map/pallas_call | solution.py:361
  42.6 0.0 copy-start
  42.6 2.9 %convert_element_type.3 = f32[8,256,256]{2,1,0:T(8,128)} convert(bf16[8,256,256]{2,1,0:T(8,128)(2,1)} %get-tuple-element.5) | non-fusion elementwise | flops 524288 | bytes 3145728 | tf_op jit(solution)/shard_map/convert_element_type | solution.py:405
  45.5 0.0 copy-done
  45.5 1.1 %copy.11 = bf16[3072,256]{1,0:T(8,128)(2,1)} copy(bf16[3072,256]{1,0:T(8,128)(2,1)S(1)} %copy-done) | data formatting | bytes 3145728
Async XLA Ops:
  42.6 2.9 %copy-start = (bf16[3072,256]{1,0:T(8,128)(2,1)S(1)}, bf16[3072,256]{1,0:T(8,128)(2,1)}, u32[]{:S(2)}) copy-start(bf16[3072,256]{1,0:T(8,128)(2,1)} %get-tuple-element.8) | copy-start | bytes 4718596

commit v3 on v2

--- a/solution.py
+++ b/solution.py
@@ -144,7 +144,7 @@
     step_rows = 512
     row_acc[...] = jnp.zeros_like(row_acc)
 
-    @pl.loop(0, table.shape[0] // step_rows)
+    @pl.loop(0, table.shape[0] // step_rows, unroll=4)
     def _(step):
         first = pl.multiple_of(step * step_rows, step_rows)
         lane = lax.broadcasted_iota(jnp.int32, (wanted.shape[0], step_rows), 1) + first
@@ -229,7 +229,7 @@
             return tuple(totals)
 
         zero = jnp.zeros(op_in.shape[2:], jnp.float32)
-        totals = lax.fori_loop(0, devices, add, (zero,) * relations)
+        totals = lax.fori_loop(0, devices, add, (zero,) * relations, unroll=4)
         for relation in range(relations):
             gathered[my_reducer, relation] = (totals[relation] * scale).astype(jnp.bfloat16)
 

time: 46.8 us -> 45.4 us (0.970)
  Pallas kernels: 42 us -> 40.6 us
    pallas_call x1, Pallas kernels: 42 us -> 40.6 us  [shards(): pl.pallas_call(functools.partial(kernel, n_rows, n_rep, scale), out_shape...]
where the time goes in v3:
time: 45.4 us; the launch traced here: 45.3 us
  Pallas kernels  40.6 us (89%)
  other arithmetic  2.85 us (6%)
  local copies, waits for them, and re-layouts  1.15 us (3%)
  between operations  0.65 us (1%)
    pallas_call x1, Pallas kernels, shards(): pl.pallas_call(functools.partial(kernel, n_rows, n_rep, scale), out_shape...  40.6 us
    convert_element_type x1, other arithmetic, shards(): return (entity_grad, relation_grad.astype(jnp.float32))  2.85 us
    unnamed x3, local copies, waits for them, and re-layouts  1.15 us

profile of v3, /device:TPU:1, one launch (start us, length us, event | category | flops | bytes accessed | tf_op | source)
XLA Modules:
  0.0 45.3 jit_solution(14962976804814274472)
XLA Ops:
  0.6 40.6 %shard_map.95 = (bf16[3072,256]{1,0:T(8,128)(2,1)}, bf16[8,256,256]{2,1,0:T(8,128)(2,1)}) custom-call(s32[2]{0:T(128)} %bitcast.12, s32[17]{0:T(128)} %bitcast.13, s32[8,16]{1,0:T(8,128)} %bitcast.11, s32[2,1024]{1,0:T(2,128)} %bitcast.8, s32[2,1024]{1,0:T(2,128)} %bitcast.9, s32[2,1024]{1,0:T(2,128)} %bitcast.10, bf16[6144,256]{1,0:T(8,128)(2,1)} %table_hbm.1, ...), custom_call_target="tpu_custom_call" | custom-call | tf_op jit(solution)/shard_map/pallas_call | solution.py:361
  41.2 0.0 copy-start
  41.3 2.9 %convert_element_type.3 = f32[8,256,256]{2,1,0:T(8,128)} convert(bf16[8,256,256]{2,1,0:T(8,128)(2,1)} %get-tuple-element.5) | non-fusion elementwise | flops 524288 | bytes 3145728 | tf_op jit(solution)/shard_map/convert_element_type | solution.py:405
  44.1 0.0 copy-done
  44.1 1.1 %copy.11 = bf16[3072,256]{1,0:T(8,128)(2,1)} copy(bf16[3072,256]{1,0:T(8,128)(2,1)S(1)} %copy-done) | data formatting | bytes 3145728
Async XLA Ops:
  41.2 2.9 %copy-start = (bf16[3072,256]{1,0:T(8,128)(2,1)S(1)}, bf16[3072,256]{1,0:T(8,128)(2,1)}, u32[]{:S(2)}) copy-start(bf16[3072,256]{1,0:T(8,128)(2,1)} %get-tuple-element.8) | copy-start | bytes 4718596

commit v4 on v3

--- a/solution.py
+++ b/solution.py
@@ -246,21 +246,6 @@
 
         remote(piece, piece, fan_sem.at[0], gather_sem.at[my_reducer], my_row, other_rep).start()
 
-    settle(grad_in, receive_sem.at[4])
-    all_rows = column(requests[...], 0).astype(jnp.int32)
-    grads = unpack(grad_in[...]).astype(jnp.bfloat16)
-    half = entity_ref.shape[0]
-
-    @pl.loop(0, half // step_rows)
-    def _(step):
-        first = pl.multiple_of(step * step_rows, step_rows)
-        lane = lax.broadcasted_iota(jnp.int32, (all_rows.shape[0], step_rows), 1) + first + my_rep * half
-        place = (all_rows == lane).astype(jnp.float32).astype(jnp.bfloat16)
-        entity_ref[pl.ds(first, step_rows), :] = dot(place, grads, 0, 0).astype(jnp.bfloat16)
-
-    entity_copy = pltpu.make_async_copy(entity_ref, entity_hbm, local_sem.at[6])
-    entity_copy.start()
-
     def mine(reducer):
         device = reducer * stride
         same_rep = lax.rem(device, n_rep) == my_rep
@@ -281,6 +266,21 @@
                 row = lax.div(my_row, PLANE) * PLANE + lax.rem(my_row + hop, PLANE)
                 remote(piece, piece, pass_sem.at[reducer, hop], gather_sem.at[reducer], row, my_rep).start()
             remote(piece, piece, pass_sem.at[reducer, 0], gather_sem.at[reducer], my_row, other_rep).start()
+
+    settle(grad_in, receive_sem.at[4])
+    all_rows = column(requests[...], 0).astype(jnp.int32)
+    grads = unpack(grad_in[...]).astype(jnp.bfloat16)
+    half = entity_ref.shape[0]
+
+    @pl.loop(0, half // step_rows, unroll=2)
+    def _(step):
+        first = pl.multiple_of(step * step_rows, step_rows)
+        lane = lax.broadcasted_iota(jnp.int32, (all_rows.shape[0], step_rows), 1) + first + my_rep * half
+        place = (all_rows == lane).astype(jnp.float32).astype(jnp.bfloat16)
+        entity_ref[pl.ds(first, step_rows), :] = dot(place, grads, 0, 0).astype(jnp.bfloat16)
+
+    entity_copy = pltpu.make_async_copy(entity_ref, entity_hbm, local_sem.at[6])
+    entity_copy.start()
 
     @pl.loop(0, reducers)
     def _(step):

time: 45.4 us -> 45.3 us (level)
  no operation moved by 1% of the time
where the time goes in v4:
time: 45.3 us; the launch traced here: 45.1 us
  Pallas kernels  40.5 us (89%)
  other arithmetic  2.85 us (6%)
  local copies, waits for them, and re-layouts  1.15 us (3%)
  between operations  0.65 us (1%)
    pallas_call x1, Pallas kernels, shards(): pl.pallas_call(functools.partial(kernel, n_rows, n_rep, scale), out_shape...  40.5 us
    convert_element_type x1, other arithmetic, shards(): return (entity_grad, relation_grad.astype(jnp.float32))  2.85 us
    unnamed x3, local copies, waits for them, and re-layouts  1.15 us

profile of v4, /device:TPU:1, one launch (start us, length us, event | category | flops | bytes accessed | tf_op | source)
XLA Modules:
  0.0 45.1 jit_solution(11431757743882715133)
XLA Ops:
  0.6 40.5 %shard_map.95 = (bf16[3072,256]{1,0:T(8,128)(2,1)}, bf16[8,256,256]{2,1,0:T(8,128)(2,1)}) custom-call(s32[2]{0:T(128)} %bitcast.12, s32[17]{0:T(128)} %bitcast.13, s32[8,16]{1,0:T(8,128)} %bitcast.11, s32[2,1024]{1,0:T(2,128)} %bitcast.8, s32[2,1024]{1,0:T(2,128)} %bitcast.9, s32[2,1024]{1,0:T(2,128)} %bitcast.10, bf16[6144,256]{1,0:T(8,128)(2,1)} %table_hbm.1, ...), custom_call_target="tpu_custom_call" | custom-call | tf_op jit(solution)/shard_map/pallas_call | solution.py:361
  41.1 0.0 copy-start
  41.1 2.9 %convert_element_type.3 = f32[8,256,256]{2,1,0:T(8,128)} convert(bf16[8,256,256]{2,1,0:T(8,128)(2,1)} %get-tuple-element.5) | non-fusion elementwise | flops 524288 | bytes 3145728 | tf_op jit(solution)/shard_map/convert_element_type | solution.py:405
  44.0 0.0 copy-done
  44.0 1.1 %copy.11 = bf16[3072,256]{1,0:T(8,128)(2,1)} copy(bf16[3072,256]{1,0:T(8,128)(2,1)S(1)} %copy-done) | data formatting | bytes 3145728
Async XLA Ops:
  41.1 2.9 %copy-start = (bf16[3072,256]{1,0:T(8,128)(2,1)S(1)}, bf16[3072,256]{1,0:T(8,128)(2,1)}, u32[]{:S(2)}) copy-start(bf16[3072,256]{1,0:T(8,128)(2,1)} %get-tuple-element.8) | copy-start | bytes 4718596

commit v5 on v4

--- a/solution.py
+++ b/solution.py
@@ -292,7 +292,7 @@
             settle(piece, gather_sem.at[reducer])
             remote(piece, piece, pass_sem.at[reducer, 0], gather_sem.at[reducer], my_row, other_rep).start()
 
-    @pl.loop(0, reducers // 2)
+    @pl.loop(0, reducers // 2, unroll=4)
     def _(pair):
         halves = []
         for reducer in (2 * pair, 2 * pair + 1):

time: 45.3 us -> 45.3 us (level)
  no operation moved by 1% of the time
where the time goes in v5:
time: 45.3 us; the launch traced here: 45.1 us
  Pallas kernels  40.5 us (89%)
  other arithmetic  2.85 us (6%)
  local copies, waits for them, and re-layouts  1.15 us (3%)
  between operations  0.65 us (1%)
    pallas_call x1, Pallas kernels, shards(): pl.pallas_call(functools.partial(kernel, n_rows, n_rep, scale), out_shape...  40.5 us
    convert_element_type x1, other arithmetic, shards(): return (entity_grad, relation_grad.astype(jnp.float32))  2.85 us
    unnamed x3, local copies, waits for them, and re-layouts  1.15 us

profile of v5, /device:TPU:1, one launch (start us, length us, event | category | flops | bytes accessed | tf_op | source)
XLA Modules:
  0.0 45.1 jit_solution(5350703179621286729)
XLA Ops:
  0.6 40.5 %shard_map.95 = (bf16[3072,256]{1,0:T(8,128)(2,1)}, bf16[8,256,256]{2,1,0:T(8,128)(2,1)}) custom-call(s32[2]{0:T(128)} %bitcast.12, s32[17]{0:T(128)} %bitcast.13, s32[8,16]{1,0:T(8,128)} %bitcast.11, s32[2,1024]{1,0:T(2,128)} %bitcast.8, s32[2,1024]{1,0:T(2,128)} %bitcast.9, s32[2,1024]{1,0:T(2,128)} %bitcast.10, bf16[6144,256]{1,0:T(8,128)(2,1)} %table_hbm.1, ...), custom_call_target="tpu_custom_call" | custom-call | tf_op jit(solution)/shard_map/pallas_call | solution.py:361
  41.1 0.0 copy-start
  41.1 2.9 %convert_element_type.3 = f32[8,256,256]{2,1,0:T(8,128)} convert(bf16[8,256,256]{2,1,0:T(8,128)(2,1)} %get-tuple-element.5) | non-fusion elementwise | flops 524288 | bytes 3145728 | tf_op jit(solution)/shard_map/convert_element_type | solution.py:405
  44.0 0.0 copy-done
  44.0 1.1 %copy.11 = bf16[3072,256]{1,0:T(8,128)(2,1)} copy(bf16[3072,256]{1,0:T(8,128)(2,1)S(1)} %copy-done) | data formatting | bytes 3145728
Async XLA Ops:
  41.1 2.9 %copy-start = (bf16[3072,256]{1,0:T(8,128)(2,1)S(1)}, bf16[3072,256]{1,0:T(8,128)(2,1)}, u32[]{:S(2)}) copy-start(bf16[3072,256]{1,0:T(8,128)(2,1)} %get-tuple-element.8) | copy-start | bytes 4718596
